TPU v7x, 32 devices: a whole 2x2x4 slice. The times are simulated.
32 devices in a mesh: stack: 8 (over y, x, core), rows: 4 (over z).
Axes of the slice: x: 2, y: 2, z: 4, core: 2. Of those that a mesh axis runs over, the one named last changes fastest.
Arguments:
- field: float32 [2, 32, 64, 1536], P(None, 'stack', 'rows'), may hold values from -6 to 6
- hess_xx: float32 [32, 64, 1536], P('stack', 'rows'), may hold values from 0.3 to 1.5
- hess_yy: float32 [32, 64, 1536], P('stack', 'rows'), may hold values from 0.3 to 1.5
- hess_xy: float32 [32, 64, 1536], P('stack', 'rows'), may hold values from -1 to 1
- gradient: float32 [2, 32, 64, 1536], P(None, 'stack', 'rows'), may hold values from -5.5 to 5.5
Outputs:
- updated: float32 [2, 32, 64, 1536], P(None, 'stack', 'rows')
All inputs are finite; a program needn't handle non-finite values.
Results may differ from a plain program's by a relative error of at most 0.00002.
Values sent between devices are 32-bit elements; how exact they have to be, the bound alone decides.
A program may use at most 64 MiB of HBM per device.

v0:
```python
import jax
import jax.numpy as jnp
from jax import lax
from jax.sharding import PartitionSpec as P

SWEEPS = 6


near_weight = 1.0
far_weight = 0.5
plane_weight = 1.0
diag_shift = 7.0


def padded_2(cells, sides, width):
    for axis, dim in sides:
        count = lax.axis_size(axis)
        ends = count - 1
        head = lax.slice_in_dim(cells, 0, width, axis=dim)
        tail = lax.slice_in_dim(cells, cells.shape[dim] - width, cells.shape[dim], axis=dim)
        cells = jnp.concatenate(
            [
                lax.ppermute(tail, axis, [(i, (i + 1) % count) for i in range(ends)]),
                cells,
                lax.ppermute(head, axis, [((i + 1) % count, i) for i in range(ends)]),
            ],
            axis=dim,
        )
    return cells


def local_sweep(sec_ext, row_ext, hess_xx, hess_yy, hess_xy, gradient):
    near = sec_ext[:, 1:-3] + sec_ext[:, 3:-1]
    far = sec_ext[:, :-4] + sec_ext[:, 4:]
    middle = row_ext[:, :, 1:-1]
    padded = jnp.pad(middle, ((0, 0), (0, 0), (0, 0), (1, 1)))
    plane = row_ext[:, :, :-2] + row_ext[:, :, 2:] + padded[:, :, :, :-2] + padded[:, :, :, 2:]
    right = -gradient + near_weight * near + far_weight * far + plane_weight * plane
    diag_a = hess_xx + diag_shift
    diag_c = hess_yy + diag_shift
    determ = diag_a * diag_c - hess_xy * hess_xy
    new_x = (diag_c * right[0] - hess_xy * right[1]) / determ
    new_y = (diag_a * right[1] - hess_xy * right[0]) / determ
    return jnp.stack([new_x, new_y])


def on_device(field, hess_xx, hess_yy, hess_xy, gradient):
    current = field
    for step in range(SWEEPS):
        sec_ext = padded_2(current, (("stack", 1),), 2)
        row_ext = padded_2(current, (("rows", 2),), 1)
        current = local_sweep(sec_ext, row_ext, hess_xx, hess_yy, hess_xy, gradient)
    return current


def solution(mesh):
    in_specs = (
        P(None, "stack", "rows", None),
        P("stack", "rows", None),
        P("stack", "rows", None),
        P("stack", "rows", None),
        P(None, "stack", "rows", None),
    )
    out_specs = P(None, "stack", "rows", None)
    return jax.shard_map(
        on_device, mesh=mesh, in_specs=in_specs, out_specs=out_specs, check_vma=False
    )
```

profile of v0, /device:TPU:1, one launch (start us, length us, event | category | flops | bytes accessed | tf_op | source)
XLA Modules:
  0.0 100.2 jit_solution(5776641807859010391)
XLA Ops:
  1.3 4.5 %collective-permute-start = (f32[2,2,16,1536]{3,2,1,0:T(8,128)S(1)}, f32[2,2,16,1536]{3,2,1,0:T(8,128)S(1)}, u32[]{:S(2)}, u32[]{:S(2)}) collective-permute-start(f32[2,2,16,1536]{3,2,1,0:T(8,128)S(1)} %get-tuple-element.49), channel_id=1, source_target_pairs={{0,4},{4,8},{8,12},{12,16},{16,20},{20,24},{24,28},{1,5},{5,9},{9,... | collective-permute-start | bytes 1179656 | tf_op jit(solution)/shard_map/ppermute | solution.py:23
  5.8 1.9 %collective-permute-start.1 = (f32[2,2,16,1536]{3,2,1,0:T(8,128)S(1)}, f32[2,2,16,1536]{3,2,1,0:T(8,128)S(1)}, u32[]{:S(2)}, u32[]{:S(2)}) collective-permute-start(f32[2,2,16,1536]{3,2,1,0:T(8,128)S(1)} %get-tuple-element.50), channel_id=1, source_target_pairs={{4,0},{8,4},{12,8},{16,12},{20,16},{24,20},{28,24},{5,1},{9,5},{13... | collective-permute-start | bytes 1179656 | tf_op jit(solution)/shard_map/ppermute | solution.py:25
  7.8 3.2 %collective-permute-start.2 = (f32[2,4,1,1536]{3,2,1,0:T(1,128)S(1)}, f32[2,4,1,1536]{3,2,1,0:T(1,128)S(1)}, u32[]{:S(2)}, u32[]{:S(2)}) collective-permute-start(f32[2,4,1,1536]{3,2,1,0:T(1,128)S(1)} %get-tuple-element.51), channel_id=1, source_target_pairs={{0,1},{1,2},{2,3},{4,5},{5,6},{6,7},{8,9},{9,10},{10,11},{12,13},{... | collective-permute-start | bytes 147464 | tf_op jit(solution)/shard_map/ppermute | solution.py:23
  12.6 3.8 %collective-permute-done.1 = f32[2,2,16,1536]{3,2,1,0:T(8,128)S(1)} collective-permute-done((f32[2,2,16,1536]{3,2,1,0:T(8,128)S(1)}, f32[2,2,16,1536]{3,2,1,0:T(8,128)S(1)}, u32[]{:S(2)}, u32[]{:S(2)}) %collective-permute-start.1) | collective-permute-done | bytes 393248 | tf_op jit(solution)/shard_map/ppermute | solution.py:25
  17.9 4.5 %collective-permute-start.4 = (f32[2,2,16,1536]{3,2,1,0:T(8,128)S(1)}, f32[2,2,16,1536]{3,2,1,0:T(8,128)S(1)}, u32[]{:S(2)}, u32[]{:S(2)}) collective-permute-start(f32[2,2,16,1536]{3,2,1,0:T(8,128)S(1)} %get-tuple-element.43), channel_id=1, source_target_pairs={{0,4},{4,8},{8,12},{12,16},{16,20},{20,24},{24,28},{1,5},{5,9},{9,... | collective-permute-start | bytes 1179656 | tf_op jit(solution)/shard_map/ppermute | solution.py:23
  22.4 1.9 %collective-permute-start.5 = (f32[2,2,16,1536]{3,2,1,0:T(8,128)S(1)}, f32[2,2,16,1536]{3,2,1,0:T(8,128)S(1)}, u32[]{:S(2)}, u32[]{:S(2)}) collective-permute-start(f32[2,2,16,1536]{3,2,1,0:T(8,128)S(1)} %get-tuple-element.44), channel_id=1, source_target_pairs={{4,0},{8,4},{12,8},{16,12},{20,16},{24,20},{28,24},{5,1},{9,5},{13... | collective-permute-start | bytes 1179656 | tf_op jit(solution)/shard_map/ppermute | solution.py:25
  24.4 3.2 %collective-permute-start.6 = (f32[2,4,1,1536]{3,2,1,0:T(1,128)S(1)}, f32[2,4,1,1536]{3,2,1,0:T(1,128)S(1)}, u32[]{:S(2)}, u32[]{:S(2)}) collective-permute-start(f32[2,4,1,1536]{3,2,1,0:T(1,128)S(1)} %get-tuple-element.45), channel_id=1, source_target_pairs={{0,1},{1,2},{2,3},{4,5},{5,6},{6,7},{8,9},{9,10},{10,11},{12,13},{... | collective-permute-start | bytes 147464 | tf_op jit(solution)/shard_map/ppermute | solution.py:23
  29.0 4.9 %collective-permute-done.5 = f32[2,2,16,1536]{3,2,1,0:T(8,128)S(1)} collective-permute-done((f32[2,2,16,1536]{3,2,1,0:T(8,128)S(1)}, f32[2,2,16,1536]{3,2,1,0:T(8,128)S(1)}, u32[]{:S(2)}, u32[]{:S(2)}) %collective-permute-start.5) | collective-permute-done | bytes 393248 | tf_op jit(solution)/shard_map/ppermute | solution.py:25
  35.0 3.4 %collective-permute-start.8 = (f32[2,2,16,1536]{3,2,1,0:T(8,128)S(1)}, f32[2,2,16,1536]{3,2,1,0:T(8,128)S(1)}, u32[]{:S(2)}, u32[]{:S(2)}) collective-permute-start(f32[2,2,16,1536]{3,2,1,0:T(8,128)S(1)} %get-tuple-element.37), channel_id=1, source_target_pairs={{0,4},{4,8},{8,12},{12,16},{16,20},{20,24},{24,28},{1,5},{5,9},{9,... | collective-permute-start | bytes 1179656 | tf_op jit(solution)/shard_map/ppermute | solution.py:23
  38.4 1.9 %collective-permute-start.9 = (f32[2,2,16,1536]{3,2,1,0:T(8,128)S(1)}, f32[2,2,16,1536]{3,2,1,0:T(8,128)S(1)}, u32[]{:S(2)}, u32[]{:S(2)}) collective-permute-start(f32[2,2,16,1536]{3,2,1,0:T(8,128)S(1)} %get-tuple-element.38), channel_id=1, source_target_pairs={{4,0},{8,4},{12,8},{16,12},{20,16},{24,20},{28,24},{5,1},{9,5},{13... | collective-permute-start | bytes 1179656 | tf_op jit(solution)/shard_map/ppermute | solution.py:25
  40.4 3.2 %collective-permute-start.10 = (f32[2,4,1,1536]{3,2,1,0:T(1,128)S(1)}, f32[2,4,1,1536]{3,2,1,0:T(1,128)S(1)}, u32[]{:S(2)}, u32[]{:S(2)}) collective-permute-start(f32[2,4,1,1536]{3,2,1,0:T(1,128)S(1)} %get-tuple-element.39), channel_id=1, source_target_pairs={{0,1},{1,2},{2,3},{4,5},{5,6},{6,7},{8,9},{9,10},{10,11},{12,13},{... | collective-permute-start | bytes 147464 | tf_op jit(solution)/shard_map/ppermute | solution.py:23
  45.0 5.7 %collective-permute-done.9 = f32[2,2,16,1536]{3,2,1,0:T(8,128)S(1)} collective-permute-done((f32[2,2,16,1536]{3,2,1,0:T(8,128)S(1)}, f32[2,2,16,1536]{3,2,1,0:T(8,128)S(1)}, u32[]{:S(2)}, u32[]{:S(2)}) %collective-permute-start.9) | collective-permute-done | bytes 393248 | tf_op jit(solution)/shard_map/ppermute | solution.py:25
  51.9 2.7 %collective-permute-start.12 = (f32[2,2,16,1536]{3,2,1,0:T(8,128)S(1)}, f32[2,2,16,1536]{3,2,1,0:T(8,128)S(1)}, u32[]{:S(2)}, u32[]{:S(2)}) collective-permute-start(f32[2,2,16,1536]{3,2,1,0:T(8,128)S(1)} %get-tuple-element.31), channel_id=1, source_target_pairs={{0,4},{4,8},{8,12},{12,16},{16,20},{20,24},{24,28},{1,5},{5,9},{9,... | collective-permute-start | bytes 1179656 | tf_op jit(solution)/shard_map/ppermute | solution.py:23
  54.7 1.9 %collective-permute-start.13 = (f32[2,2,16,1536]{3,2,1,0:T(8,128)S(1)}, f32[2,2,16,1536]{3,2,1,0:T(8,128)S(1)}, u32[]{:S(2)}, u32[]{:S(2)}) collective-permute-start(f32[2,2,16,1536]{3,2,1,0:T(8,128)S(1)} %get-tuple-element.32), channel_id=1, source_target_pairs={{4,0},{8,4},{12,8},{16,12},{20,16},{24,20},{28,24},{5,1},{9,5},{13... | collective-permute-start | bytes 1179656 | tf_op jit(solution)/shard_map/ppermute | solution.py:25
  56.7 2.9 %collective-permute-start.14 = (f32[2,4,1,1536]{3,2,1,0:T(1,128)S(1)}, f32[2,4,1,1536]{3,2,1,0:T(1,128)S(1)}, u32[]{:S(2)}, u32[]{:S(2)}) collective-permute-start(f32[2,4,1,1536]{3,2,1,0:T(1,128)S(1)} %get-tuple-element.33), channel_id=1, source_target_pairs={{0,1},{1,2},{2,3},{4,5},{5,6},{6,7},{8,9},{9,10},{10,11},{12,13},{... | collective-permute-start | bytes 147464 | tf_op jit(solution)/shard_map/ppermute | solution.py:23
  60.9 6.7 %collective-permute-done.13 = f32[2,2,16,1536]{3,2,1,0:T(8,128)S(1)} collective-permute-done((f32[2,2,16,1536]{3,2,1,0:T(8,128)S(1)}, f32[2,2,16,1536]{3,2,1,0:T(8,128)S(1)}, u32[]{:S(2)}, u32[]{:S(2)}) %collective-permute-start.13) | collective-permute-done | bytes 393248 | tf_op jit(solution)/shard_map/ppermute | solution.py:25
  68.8 1.9 %collective-permute-start.16 = (f32[2,2,16,1536]{3,2,1,0:T(8,128)S(1)}, f32[2,2,16,1536]{3,2,1,0:T(8,128)S(1)}, u32[]{:S(2)}, u32[]{:S(2)}) collective-permute-start(f32[2,2,16,1536]{3,2,1,0:T(8,128)S(1)} %get-tuple-element.25), channel_id=1, source_target_pairs={{0,4},{4,8},{8,12},{12,16},{16,20},{20,24},{24,28},{1,5},{5,9},{9,... | collective-permute-start | bytes 1179656 | tf_op jit(solution)/shard_map/ppermute | solution.py:23
  70.7 2.4 %collective-permute-start.17 = (f32[2,2,16,1536]{3,2,1,0:T(8,128)S(1)}, f32[2,2,16,1536]{3,2,1,0:T(8,128)S(1)}, u32[]{:S(2)}, u32[]{:S(2)}) collective-permute-start(f32[2,2,16,1536]{3,2,1,0:T(8,128)S(1)} %get-tuple-element.26), channel_id=1, source_target_pairs={{4,0},{8,4},{12,8},{16,12},{20,16},{24,20},{28,24},{5,1},{9,5},{13... | collective-permute-start | bytes 1179656 | tf_op jit(solution)/shard_map/ppermute | solution.py:25
  73.2 1.6 %collective-permute-start.18 = (f32[2,4,1,1536]{3,2,1,0:T(1,128)S(1)}, f32[2,4,1,1536]{3,2,1,0:T(1,128)S(1)}, u32[]{:S(2)}, u32[]{:S(2)}) collective-permute-start(f32[2,4,1,1536]{3,2,1,0:T(1,128)S(1)} %get-tuple-element.27), channel_id=1, source_target_pairs={{0,1},{1,2},{2,3},{4,5},{5,6},{6,7},{8,9},{9,10},{10,11},{12,13},{... | collective-permute-start | bytes 147464 | tf_op jit(solution)/shard_map/ppermute | solution.py:23
  76.2 6.7 %collective-permute-done.17 = f32[2,2,16,1536]{3,2,1,0:T(8,128)S(1)} collective-permute-done((f32[2,2,16,1536]{3,2,1,0:T(8,128)S(1)}, f32[2,2,16,1536]{3,2,1,0:T(8,128)S(1)}, u32[]{:S(2)}, u32[]{:S(2)}) %collective-permute-start.17) | collective-permute-done | bytes 393248 | tf_op jit(solution)/shard_map/ppermute | solution.py:25
  84.1 1.9 %collective-permute-start.20 = (f32[2,2,16,1536]{3,2,1,0:T(8,128)S(1)}, f32[2,2,16,1536]{3,2,1,0:T(8,128)S(1)}, u32[]{:S(2)}, u32[]{:S(2)}) collective-permute-start(f32[2,2,16,1536]{3,2,1,0:T(8,128)S(1)} %get-tuple-element.19), channel_id=1, source_target_pairs={{0,4},{4,8},{8,12},{12,16},{16,20},{20,24},{24,28},{1,5},{5,9},{9,... | collective-permute-start | bytes 1179656 | tf_op jit(solution)/shard_map/ppermute | solution.py:23
  86.0 2.4 %collective-permute-start.21 = (f32[2,2,16,1536]{3,2,1,0:T(8,128)S(1)}, f32[2,2,16,1536]{3,2,1,0:T(8,128)S(1)}, u32[]{:S(2)}, u32[]{:S(2)}) collective-permute-start(f32[2,2,16,1536]{3,2,1,0:T(8,128)S(1)} %get-tuple-element.20), channel_id=1, source_target_pairs={{4,0},{8,4},{12,8},{16,12},{20,16},{24,20},{28,24},{5,1},{9,5},{13... | collective-permute-start | bytes 1179656 | tf_op jit(solution)/shard_map/ppermute | solution.py:25
  88.5 1.6 %collective-permute-start.22 = (f32[2,4,1,1536]{3,2,1,0:T(1,128)S(1)}, f32[2,4,1,1536]{3,2,1,0:T(1,128)S(1)}, u32[]{:S(2)}, u32[]{:S(2)}) collective-permute-start(f32[2,4,1,1536]{3,2,1,0:T(1,128)S(1)} %get-tuple-element.21), channel_id=1, source_target_pairs={{0,1},{1,2},{2,3},{4,5},{5,6},{6,7},{8,9},{9,10},{10,11},{12,13},{... | collective-permute-start | bytes 147464 | tf_op jit(solution)/shard_map/ppermute | solution.py:23
  91.6 6.7 %collective-permute-done.21 = f32[2,2,16,1536]{3,2,1,0:T(8,128)S(1)} collective-permute-done((f32[2,2,16,1536]{3,2,1,0:T(8,128)S(1)}, f32[2,2,16,1536]{3,2,1,0:T(8,128)S(1)}, u32[]{:S(2)}, u32[]{:S(2)}) %collective-permute-start.21) | collective-permute-done | bytes 393248 | tf_op jit(solution)/shard_map/ppermute | solution.py:25
  (74 shorter events, 17.8 us)
Async XLA Ops:
  1.3 11.1 %collective-permute-start = (f32[2,2,16,1536]{3,2,1,0:T(8,128)S(1)}, f32[2,2,16,1536]{3,2,1,0:T(8,128)S(1)}, u32[]{:S(2)}, u32[]{:S(2)}) collective-permute-start(f32[2,2,16,1536]{3,2,1,0:T(8,128)S(1)} %get-tuple-element.49), channel_id=1, source_target_pairs={{0,4},{4,8},{8,12},{12,16},{16,20},{20,24},{24,28},{1,5},{5,9},{9,... | collective-permute-start | bytes 1179656 | tf_op jit(solution)/shard_map/ppermute | solution.py:23
  5.8 10.6 %collective-permute-start.1 = (f32[2,2,16,1536]{3,2,1,0:T(8,128)S(1)}, f32[2,2,16,1536]{3,2,1,0:T(8,128)S(1)}, u32[]{:S(2)}, u32[]{:S(2)}) collective-permute-start(f32[2,2,16,1536]{3,2,1,0:T(8,128)S(1)} %get-tuple-element.50), channel_id=1, source_target_pairs={{4,0},{8,4},{12,8},{16,12},{20,16},{24,20},{28,24},{5,1},{9,5},{13... | collective-permute-start | bytes 1179656 | tf_op jit(solution)/shard_map/ppermute | solution.py:25
  7.8 8.6 %collective-permute-start.2 = (f32[2,4,1,1536]{3,2,1,0:T(1,128)S(1)}, f32[2,4,1,1536]{3,2,1,0:T(1,128)S(1)}, u32[]{:S(2)}, u32[]{:S(2)}) collective-permute-start(f32[2,4,1,1536]{3,2,1,0:T(1,128)S(1)} %get-tuple-element.51), channel_id=1, source_target_pairs={{0,1},{1,2},{2,3},{4,5},{5,6},{6,7},{8,9},{9,10},{10,11},{12,13},{... | collective-permute-start | bytes 147464 | tf_op jit(solution)/shard_map/ppermute | solution.py:23
  11.0 5.4 %collective-permute-start.3 = (f32[2,4,1,1536]{3,2,1,0:T(1,128)S(1)}, f32[2,4,1,1536]{3,2,1,0:T(1,128)S(1)}, u32[]{:S(2)}, u32[]{:S(2)}) collective-permute-start(f32[2,4,1,1536]{3,2,1,0:T(1,128)S(1)} %get-tuple-element.52), channel_id=1, source_target_pairs={{1,0},{2,1},{3,2},{5,4},{6,5},{7,6},{9,8},{10,9},{11,10},{13,12},{... | collective-permute-start | bytes 147464 | tf_op jit(solution)/shard_map/ppermute | solution.py:25
  17.9 11.1 %collective-permute-start.4 = (f32[2,2,16,1536]{3,2,1,0:T(8,128)S(1)}, f32[2,2,16,1536]{3,2,1,0:T(8,128)S(1)}, u32[]{:S(2)}, u32[]{:S(2)}) collective-permute-start(f32[2,2,16,1536]{3,2,1,0:T(8,128)S(1)} %get-tuple-element.43), channel_id=1, source_target_pairs={{0,4},{4,8},{8,12},{12,16},{16,20},{20,24},{24,28},{1,5},{5,9},{9,... | collective-permute-start | bytes 1179656 | tf_op jit(solution)/shard_map/ppermute | solution.py:23
  22.4 11.5 %collective-permute-start.5 = (f32[2,2,16,1536]{3,2,1,0:T(8,128)S(1)}, f32[2,2,16,1536]{3,2,1,0:T(8,128)S(1)}, u32[]{:S(2)}, u32[]{:S(2)}) collective-permute-start(f32[2,2,16,1536]{3,2,1,0:T(8,128)S(1)} %get-tuple-element.44), channel_id=1, source_target_pairs={{4,0},{8,4},{12,8},{16,12},{20,16},{24,20},{28,24},{5,1},{9,5},{13... | collective-permute-start | bytes 1179656 | tf_op jit(solution)/shard_map/ppermute | solution.py:25
  24.4 9.8 %collective-permute-start.6 = (f32[2,4,1,1536]{3,2,1,0:T(1,128)S(1)}, f32[2,4,1,1536]{3,2,1,0:T(1,128)S(1)}, u32[]{:S(2)}, u32[]{:S(2)}) collective-permute-start(f32[2,4,1,1536]{3,2,1,0:T(1,128)S(1)} %get-tuple-element.45), channel_id=1, source_target_pairs={{0,1},{1,2},{2,3},{4,5},{5,6},{6,7},{8,9},{9,10},{10,11},{12,13},{... | collective-permute-start | bytes 147464 | tf_op jit(solution)/shard_map/ppermute | solution.py:23
  27.6 6.6 %collective-permute-start.7 = (f32[2,4,1,1536]{3,2,1,0:T(1,128)S(1)}, f32[2,4,1,1536]{3,2,1,0:T(1,128)S(1)}, u32[]{:S(2)}, u32[]{:S(2)}) collective-permute-start(f32[2,4,1,1536]{3,2,1,0:T(1,128)S(1)} %get-tuple-element.46), channel_id=1, source_target_pairs={{1,0},{2,1},{3,2},{5,4},{6,5},{7,6},{9,8},{10,9},{11,10},{13,12},{... | collective-permute-start | bytes 147464 | tf_op jit(solution)/shard_map/ppermute | solution.py:25
  35.0 10.0 %collective-permute-start.8 = (f32[2,2,16,1536]{3,2,1,0:T(8,128)S(1)}, f32[2,2,16,1536]{3,2,1,0:T(8,128)S(1)}, u32[]{:S(2)}, u32[]{:S(2)}) collective-permute-start(f32[2,2,16,1536]{3,2,1,0:T(8,128)S(1)} %get-tuple-element.37), channel_id=1, source_target_pairs={{0,4},{4,8},{8,12},{12,16},{16,20},{20,24},{24,28},{1,5},{5,9},{9,... | collective-permute-start | bytes 1179656 | tf_op jit(solution)/shard_map/ppermute | solution.py:23
  38.4 12.3 %collective-permute-start.9 = (f32[2,2,16,1536]{3,2,1,0:T(8,128)S(1)}, f32[2,2,16,1536]{3,2,1,0:T(8,128)S(1)}, u32[]{:S(2)}, u32[]{:S(2)}) collective-permute-start(f32[2,2,16,1536]{3,2,1,0:T(8,128)S(1)} %get-tuple-element.38), channel_id=1, source_target_pairs={{4,0},{8,4},{12,8},{16,12},{20,16},{24,20},{28,24},{5,1},{9,5},{13... | collective-permute-start | bytes 1179656 | tf_op jit(solution)/shard_map/ppermute | solution.py:25
  40.4 10.6 %collective-permute-start.10 = (f32[2,4,1,1536]{3,2,1,0:T(1,128)S(1)}, f32[2,4,1,1536]{3,2,1,0:T(1,128)S(1)}, u32[]{:S(2)}, u32[]{:S(2)}) collective-permute-start(f32[2,4,1,1536]{3,2,1,0:T(1,128)S(1)} %get-tuple-element.39), channel_id=1, source_target_pairs={{0,1},{1,2},{2,3},{4,5},{5,6},{6,7},{8,9},{9,10},{10,11},{12,13},{... | collective-permute-start | bytes 147464 | tf_op jit(solution)/shard_map/ppermute | solution.py:23
  43.7 7.4 %collective-permute-start.11 = (f32[2,4,1,1536]{3,2,1,0:T(1,128)S(1)}, f32[2,4,1,1536]{3,2,1,0:T(1,128)S(1)}, u32[]{:S(2)}, u32[]{:S(2)}) collective-permute-start(f32[2,4,1,1536]{3,2,1,0:T(1,128)S(1)} %get-tuple-element.40), channel_id=1, source_target_pairs={{1,0},{2,1},{3,2},{5,4},{6,5},{7,6},{9,8},{10,9},{11,10},{13,12},{... | collective-permute-start | bytes 147464 | tf_op jit(solution)/shard_map/ppermute | solution.py:25
  51.9 9.0 %collective-permute-start.12 = (f32[2,2,16,1536]{3,2,1,0:T(8,128)S(1)}, f32[2,2,16,1536]{3,2,1,0:T(8,128)S(1)}, u32[]{:S(2)}, u32[]{:S(2)}) collective-permute-start(f32[2,2,16,1536]{3,2,1,0:T(8,128)S(1)} %get-tuple-element.31), channel_id=1, source_target_pairs={{0,4},{4,8},{8,12},{12,16},{16,20},{20,24},{24,28},{1,5},{5,9},{9,... | collective-permute-start | bytes 1179656 | tf_op jit(solution)/shard_map/ppermute | solution.py:23
  54.7 13.0 %collective-permute-start.13 = (f32[2,2,16,1536]{3,2,1,0:T(8,128)S(1)}, f32[2,2,16,1536]{3,2,1,0:T(8,128)S(1)}, u32[]{:S(2)}, u32[]{:S(2)}) collective-permute-start(f32[2,2,16,1536]{3,2,1,0:T(8,128)S(1)} %get-tuple-element.32), channel_id=1, source_target_pairs={{4,0},{8,4},{12,8},{16,12},{20,16},{24,20},{28,24},{5,1},{9,5},{13... | collective-permute-start | bytes 1179656 | tf_op jit(solution)/shard_map/ppermute | solution.py:25
  56.7 11.3 %collective-permute-start.14 = (f32[2,4,1,1536]{3,2,1,0:T(1,128)S(1)}, f32[2,4,1,1536]{3,2,1,0:T(1,128)S(1)}, u32[]{:S(2)}, u32[]{:S(2)}) collective-permute-start(f32[2,4,1,1536]{3,2,1,0:T(1,128)S(1)} %get-tuple-element.33), channel_id=1, source_target_pairs={{0,1},{1,2},{2,3},{4,5},{5,6},{6,7},{8,9},{9,10},{10,11},{12,13},{... | collective-permute-start | bytes 147464 | tf_op jit(solution)/shard_map/ppermute | solution.py:23
  59.6 8.4 %collective-permute-start.15 = (f32[2,4,1,1536]{3,2,1,0:T(1,128)S(1)}, f32[2,4,1,1536]{3,2,1,0:T(1,128)S(1)}, u32[]{:S(2)}, u32[]{:S(2)}) collective-permute-start(f32[2,4,1,1536]{3,2,1,0:T(1,128)S(1)} %get-tuple-element.34), channel_id=1, source_target_pairs={{1,0},{2,1},{3,2},{5,4},{6,5},{7,6},{9,8},{10,9},{11,10},{13,12},{... | collective-permute-start | bytes 147464 | tf_op jit(solution)/shard_map/ppermute | solution.py:25
  68.8 7.5 %collective-permute-start.16 = (f32[2,2,16,1536]{3,2,1,0:T(8,128)S(1)}, f32[2,2,16,1536]{3,2,1,0:T(8,128)S(1)}, u32[]{:S(2)}, u32[]{:S(2)}) collective-permute-start(f32[2,2,16,1536]{3,2,1,0:T(8,128)S(1)} %get-tuple-element.25), channel_id=1, source_target_pairs={{0,4},{4,8},{8,12},{12,16},{16,20},{20,24},{24,28},{1,5},{5,9},{9,... | collective-permute-start | bytes 1179656 | tf_op jit(solution)/shard_map/ppermute | solution.py:23
  70.7 12.2 %collective-permute-start.17 = (f32[2,2,16,1536]{3,2,1,0:T(8,128)S(1)}, f32[2,2,16,1536]{3,2,1,0:T(8,128)S(1)}, u32[]{:S(2)}, u32[]{:S(2)}) collective-permute-start(f32[2,2,16,1536]{3,2,1,0:T(8,128)S(1)} %get-tuple-element.26), channel_id=1, source_target_pairs={{4,0},{8,4},{12,8},{16,12},{20,16},{24,20},{28,24},{5,1},{9,5},{13... | collective-permute-start | bytes 1179656 | tf_op jit(solution)/shard_map/ppermute | solution.py:25
  73.2 10.0 %collective-permute-start.18 = (f32[2,4,1,1536]{3,2,1,0:T(1,128)S(1)}, f32[2,4,1,1536]{3,2,1,0:T(1,128)S(1)}, u32[]{:S(2)}, u32[]{:S(2)}) collective-permute-start(f32[2,4,1,1536]{3,2,1,0:T(1,128)S(1)} %get-tuple-element.27), channel_id=1, source_target_pairs={{0,1},{1,2},{2,3},{4,5},{5,6},{6,7},{8,9},{9,10},{10,11},{12,13},{... | collective-permute-start | bytes 147464 | tf_op jit(solution)/shard_map/ppermute | solution.py:23
  74.9 8.4 %collective-permute-start.19 = (f32[2,4,1,1536]{3,2,1,0:T(1,128)S(1)}, f32[2,4,1,1536]{3,2,1,0:T(1,128)S(1)}, u32[]{:S(2)}, u32[]{:S(2)}) collective-permute-start(f32[2,4,1,1536]{3,2,1,0:T(1,128)S(1)} %get-tuple-element.28), channel_id=1, source_target_pairs={{1,0},{2,1},{3,2},{5,4},{6,5},{7,6},{9,8},{10,9},{11,10},{13,12},{... | collective-permute-start | bytes 147464 | tf_op jit(solution)/shard_map/ppermute | solution.py:25
  84.1 7.5 %collective-permute-start.20 = (f32[2,2,16,1536]{3,2,1,0:T(8,128)S(1)}, f32[2,2,16,1536]{3,2,1,0:T(8,128)S(1)}, u32[]{:S(2)}, u32[]{:S(2)}) collective-permute-start(f32[2,2,16,1536]{3,2,1,0:T(8,128)S(1)} %get-tuple-element.19), channel_id=1, source_target_pairs={{0,4},{4,8},{8,12},{12,16},{16,20},{20,24},{24,28},{1,5},{5,9},{9,... | collective-permute-start | bytes 1179656 | tf_op jit(solution)/shard_map/ppermute | solution.py:23
  86.0 12.2 %collective-permute-start.21 = (f32[2,2,16,1536]{3,2,1,0:T(8,128)S(1)}, f32[2,2,16,1536]{3,2,1,0:T(8,128)S(1)}, u32[]{:S(2)}, u32[]{:S(2)}) collective-permute-start(f32[2,2,16,1536]{3,2,1,0:T(8,128)S(1)} %get-tuple-element.20), channel_id=1, source_target_pairs={{4,0},{8,4},{12,8},{16,12},{20,16},{24,20},{28,24},{5,1},{9,5},{13... | collective-permute-start | bytes 1179656 | tf_op jit(solution)/shard_map/ppermute | solution.py:25
  88.5 10.0 %collective-permute-start.22 = (f32[2,4,1,1536]{3,2,1,0:T(1,128)S(1)}, f32[2,4,1,1536]{3,2,1,0:T(1,128)S(1)}, u32[]{:S(2)}, u32[]{:S(2)}) collective-permute-start(f32[2,4,1,1536]{3,2,1,0:T(1,128)S(1)} %get-tuple-element.21), channel_id=1, source_target_pairs={{0,1},{1,2},{2,3},{4,5},{5,6},{6,7},{8,9},{9,10},{10,11},{12,13},{... | collective-permute-start | bytes 147464 | tf_op jit(solution)/shard_map/ppermute | solution.py:23
  90.2 8.4 %collective-permute-start.23 = (f32[2,4,1,1536]{3,2,1,0:T(1,128)S(1)}, f32[2,4,1,1536]{3,2,1,0:T(1,128)S(1)}, u32[]{:S(2)}, u32[]{:S(2)}) collective-permute-start(f32[2,4,1,1536]{3,2,1,0:T(1,128)S(1)} %get-tuple-element.22), channel_id=1, source_target_pairs={{1,0},{2,1},{3,2},{5,4},{6,5},{7,6},{9,8},{10,9},{11,10},{13,12},{... | collective-permute-start | bytes 147464 | tf_op jit(solution)/shard_map/ppermute | solution.py:25
  (6 other events, 16.0 us)
where the time goes:
time: 101 us; the launch traced here: 100 us
  starting transfers between devices  55.1 us (55%)
  waiting for transfers between devices  34.5 us (34%)
  other arithmetic  6.95 us (7%)
  local copies, waits for them, and re-layouts  3.08 us (3%)
    ppermute x12, starting transfers between devices, padded_2(): lax.ppermute(tail, axis, [(i, (i + 1) % count) for i in range(ends)])  34.8 us
    ppermute x12, waiting for transfers between devices, padded_2(): lax.ppermute(head, axis, [((i + 1) % count, i) for i in range(ends)])  34.4 us
    ppermute x12, starting transfers between devices, padded_2(): lax.ppermute(head, axis, [((i + 1) % count, i) for i in range(ends)])  20.3 us
    add x6, other arithmetic, local_sweep(): -gradient + near_weight * near + far_weight * far + plane_weight * plane  3.42 us
    another operation x22, other arithmetic, local_sweep(): return jnp.stack([new_x, new_y])  2.07 us
  transfers between devices with their start and end apart: 24, of which 6 were waited for; matrix products, arithmetic and copies ran while one was open for 2% of the time, Pallas kernels for 0%

commit v1 on v0

v1 whole, which is shorter than its diff:
```python
import functools

import jax
import jax.numpy as jnp
from jax import lax
from jax.experimental import pallas as pl
from jax.experimental.pallas import tpu as pltpu
from jax.sharding import PartitionSpec as P

SWEEPS = 6
NEAR, FAR, PLANE, SHIFT = 1.0, 0.5, 1.0, 7.0
PAD = 128
CHUNKS = 4
AHEAD = 2


def kernel(n_stack, n_rows, detour, field, hxx, hyy, hxy, grad, out,
           u, g, ca, cc, cb, row_out, row_in, passing,
           load_sem, send_sem, recv_sem, pass_send, pass_in, pass_out, pass_recv, out_sem):
    sections, height, width = hxx.shape
    cw = width // CHUNKS
    half = height // 2
    s = lax.axis_index("stack")
    z = lax.axis_index("rows")
    has_left, has_right = s > 0, s < n_stack - 1
    has_up, has_down = z > 0, z < n_rows - 1
    left, right = (s - 1, z), (s + 1, z)
    up, down = (s, z - 1), (s, z + 1)
    sides = ((has_left, left), (has_right, right), (has_up, up), (has_down, down))

    lo, hi = n_stack // 2 - 1, n_stack // 2
    is_lo, is_hi, is_first, is_last = s == lo, s == hi, s == 0, s == n_stack - 1
    via_last, via_first = (n_stack - 1, z), (0, z)

    barrier = pltpu.get_barrier_semaphore()
    expected = jnp.int32(0)
    for exists, where in sides:
        expected = expected + exists.astype(jnp.int32)

        @pl.when(exists)
        def _():
            pl.semaphore_signal(barrier, inc=1, device_id=where)
    if detour:
        for who, peers in ((is_lo, (0, n_stack - 1)), (is_hi, (0, n_stack - 1)),
                           (is_first, (lo, hi)), (is_last, (lo, hi))):
            expected = expected + 2 * who.astype(jnp.int32)

            @pl.when(who)
            def _():
                for peer in peers:
                    pl.semaphore_signal(barrier, inc=1, device_id=(peer, z))

    loads = [
        pltpu.make_async_copy(field, u.at[0, :, 2:sections + 2, :, PAD:PAD + width], load_sem.at[0]),
        pltpu.make_async_copy(hxx, ca, load_sem.at[1]),
        pltpu.make_async_copy(hyy, cc, load_sem.at[2]),
        pltpu.make_async_copy(hxy, cb, load_sem.at[3]),
        pltpu.make_async_copy(grad, g, load_sem.at[4]),
    ]
    for load in loads:
        load.start()
    pl.semaphore_wait(barrier, expected)

    def cols(c):
        return pl.ds(pl.multiple_of(c * cw + PAD, 128), cw)

    def raw_cols(c):
        return pl.ds(pl.multiple_of(c * cw, 128), cw)

    def section_copy(t, c, d, rows, first=False):
        dst = u.at[t, :, 0:2, rows, cols(c)] if d == 0 else u.at[t, :, sections + 2:sections + 4, rows, cols(c)]
        if first:
            src = field.at[:, sections - 2:sections, rows, raw_cols(c)] if d == 0 else field.at[:, 0:2, rows, raw_cols(c)]
        else:
            src = u.at[t, :, sections:sections + 2, rows, cols(c)] if d == 0 else u.at[t, :, 2:4, rows, cols(c)]
        return pltpu.make_async_remote_copy(
            src_ref=src, dst_ref=dst, send_sem=send_sem.at[t, c, d], recv_sem=recv_sem.at[t, c, d],
            device_id=right if d == 0 else left)

    def pass_copy(t, c, d, first=False):
        rows = slice(half, height)
        if first:
            src = field.at[:, sections - 2:sections, rows, raw_cols(c)] if d == 0 else field.at[:, 0:2, rows, raw_cols(c)]
        else:
            src = u.at[t, :, sections:sections + 2, rows, cols(c)] if d == 0 else u.at[t, :, 2:4, rows, cols(c)]
        return pltpu.make_async_remote_copy(
            src_ref=src, dst_ref=passing.at[t, :, :, :, raw_cols(c)], send_sem=pass_send.at[t, c],
            recv_sem=pass_in.at[t, c], device_id=via_last if d == 0 else via_first)

    def onward_copy(t, c, d):
        rows = slice(half, height)
        dst = u.at[t, :, 0:2, rows, cols(c)] if d == 0 else u.at[t, :, sections + 2:sections + 4, rows, cols(c)]
        return pltpu.make_async_remote_copy(
            src_ref=passing.at[t, :, :, :, raw_cols(c)], dst_ref=dst, send_sem=pass_out.at[t, c],
            recv_sem=pass_recv.at[t, c], device_id=(hi if d == 0 else lo, z))

    def row_copy(t, c, d):
        return pltpu.make_async_remote_copy(
            src_ref=row_out.at[t, d, :, raw_cols(c)], dst_ref=row_in.at[t, d, :, raw_cols(c)],
            send_sem=send_sem.at[t, c, 2 + d], recv_sem=recv_sem.at[t, c, 2 + d],
            device_id=down if d == 0 else up)

    def each_section_copy(t, c, do, first=False):
        every, upper = slice(0, height), slice(0, half)
        for d, exists, split in ((0, has_right, is_lo), (1, has_left, is_hi)):
            if detour:
                @pl.when(split)
                def _():
                    do(section_copy(t, c, d, upper, first), pass_copy(t, c, d, first))

                @pl.when(exists & jnp.logical_not(split))
                def _():
                    do(section_copy(t, c, d, every, first), None)
            else:
                @pl.when(exists)
                def _():
                    do(section_copy(t, c, d, every, first), None)

    def start(copy, other):
        if other is not None:
            other.start()
        copy.start()

    def finish(copy, other):
        copy.wait_send()
        if other is not None:
            other.wait_send()

    def await_sections(t, c):
        every, upper = slice(0, height), slice(0, half)
        for d, exists, split in ((0, has_left, is_hi), (1, has_right, is_lo)):
            if detour:
                @pl.when(split)
                def _():
                    section_copy(t, c, d, upper).wait_recv()
                    onward_copy(t, c, d).wait_recv()

                @pl.when(exists & jnp.logical_not(split))
                def _():
                    section_copy(t, c, d, every).wait_recv()
            else:
                @pl.when(exists)
                def _():
                    section_copy(t, c, d, every).wait_recv()

    def send_rows(t, c):
        for d, exists, edge in ((0, has_down, height - 1), (1, has_up, 0)):
            for i in range(2):
                for k in range(sections):
                    at = i * sections + k
                    row_out[t, d, at:at + 1, raw_cols(c)] = u[t, i, 2 + k, edge:edge + 1, cols(c)]

            @pl.when(exists)
            def _():
                row_copy(t, c, d).start()

    def pass_on(j):
        t, c = lax.div(j, CHUNKS), lax.rem(j, CHUNKS)
        for d, who in ((0, is_last), (1, is_first)):
            @pl.when(who)
            def _():
                pass_copy(t, c, d).wait_recv()
                onward_copy(t, c, d).start()

    def over(count, body):
        lax.fori_loop(0, count, lambda i, _: (body(i), None)[1], None)

    over(CHUNKS, lambda c: each_section_copy(0, c, start, True))

    for t in range(SWEEPS):
        for at in (0, PAD + width):
            u[t, :, 2:sections + 2, :, at:at + PAD] = jnp.zeros((2, sections, height, PAD), jnp.float32)
    def zero(t):
        for exists, at in ((has_left, 0), (has_right, sections + 2)):
            @pl.when(jnp.logical_not(exists))
            def _():
                u[t, :, at:at + 2, :, PAD:PAD + width] = jnp.zeros((2, 2, height, width), jnp.float32)
        for d, exists in ((0, has_up), (1, has_down)):
            @pl.when(jnp.logical_not(exists))
            def _():
                row_in[t, d] = jnp.zeros((2 * sections, width), jnp.float32)
    over(SWEEPS, zero)

    loads[0].wait()
    over(CHUNKS, lambda c: send_rows(0, c))
    for load in loads[1:]:
        load.wait()

    def coefficients(c):
        at = raw_cols(c)
        for k in range(sections):
            a = ca[k, :, at] + SHIFT
            c_ = cc[k, :, at] + SHIFT
            b = cb[k, :, at]
            inverse = 1.0 / (a * c_ - b * b)
            ca[k, :, at] = a * inverse
            cc[k, :, at] = c_ * inverse
            cb[k, :, at] = b * inverse
    over(CHUNKS, coefficients)

    if detour:
        over(AHEAD, pass_on)

    top = lax.broadcasted_iota(jnp.int32, (height, cw), 0) == 0
    bottom = lax.broadcasted_iota(jnp.int32, (height, cw), 0) == height - 1

    def step(i):
        t, c = lax.div(i, CHUNKS), lax.rem(i, CHUNKS)
        if detour:
            @pl.when(i + AHEAD < SWEEPS * CHUNKS)
            def _():
                pass_on(i + AHEAD)
        for d, exists in ((0, has_up), (1, has_down)):
            @pl.when(exists)
            def _():
                row_copy(t, c, d).wait_recv()
        await_sections(t, c)
        at = raw_cols(c)
        for k in range(sections):
            r = []
            for comp in range(2):
                wide = u[t, comp, 2 + k, :, pl.ds(pl.multiple_of(c * cw, 128), cw + 2 * PAD)]
                mid = wide[:, PAD:PAD + cw]
                row = comp * sections + k
                above = jnp.where(top, row_in[t, 0, row:row + 1, at], pltpu.roll(mid, 1, 0))
                below = jnp.where(bottom, row_in[t, 1, row:row + 1, at], pltpu.roll(mid, height - 1, 0))
                before = pltpu.roll(wide, 1, 1)[:, PAD:PAD + cw]
                after = pltpu.roll(wide, cw + 2 * PAD - 1, 1)[:, PAD:PAD + cw]
                near = u[t, comp, 1 + k, :, cols(c)] + u[t, comp, 3 + k, :, cols(c)]
                far = u[t, comp, k, :, cols(c)] + u[t, comp, 4 + k, :, cols(c)]
                plane = (above + below) + (before + after)
                r.append((NEAR * near + FAR * far) + (PLANE * plane - g[comp, k, :, at]))
            b = cb[k, :, at]
            u[t + 1, 0, 2 + k, :, cols(c)] = cc[k, :, at] * r[0] - b * r[1]
            u[t + 1, 1, 2 + k, :, cols(c)] = ca[k, :, at] * r[1] - b * r[0]

        @pl.when(t < SWEEPS - 1)
        def _():
            each_section_copy(t + 1, c, start)
            send_rows(t + 1, c)

    over(SWEEPS * CHUNKS, step)

    store = pltpu.make_async_copy(u.at[SWEEPS, :, 2:sections + 2, :, PAD:PAD + width], out, out_sem)
    store.start()

    def drain(i):
        t, c = lax.div(i, CHUNKS), lax.rem(i, CHUNKS)
        each_section_copy(t, c, finish)
        for d, exists in ((0, has_down), (1, has_up)):
            @pl.when(exists)
            def _():
                row_copy(t, c, d).wait_send()
        if detour:
            for d, who in ((0, is_last), (1, is_first)):
                @pl.when(who)
                def _():
                    onward_copy(t, c, d).wait_send()
    over(SWEEPS * CHUNKS, drain)
    store.wait()


def on_device(n_stack, n_rows, field, hess_xx, hess_yy, hess_xy, gradient):
    sections, height, width = hess_xx.shape
    detour = n_stack == 8
    f32 = jnp.float32
    dma = pltpu.SemaphoreType.DMA
    return pl.pallas_call(
        functools.partial(kernel, n_stack, n_rows, detour),
        out_shape=jax.ShapeDtypeStruct(field.shape, f32),
        in_specs=[pl.BlockSpec(memory_space=pl.ANY)] * 5,
        out_specs=pl.BlockSpec(memory_space=pl.ANY),
        scratch_shapes=[
            pltpu.VMEM((SWEEPS + 1, 2, sections + 4, height, width + 2 * PAD), f32),
            pltpu.VMEM((2, sections, height, width), f32),
            pltpu.VMEM((sections, height, width), f32),
            pltpu.VMEM((sections, height, width), f32),
            pltpu.VMEM((sections, height, width), f32),
            pltpu.VMEM((SWEEPS, 2, 2 * sections, width), f32),
            pltpu.VMEM((SWEEPS, 2, 2 * sections, width), f32),
            pltpu.VMEM((SWEEPS, 2, 2, height // 2, width), f32),
            dma((5,)),
            dma((SWEEPS, CHUNKS, 4)),
            dma((SWEEPS, CHUNKS, 4)),
            dma((SWEEPS, CHUNKS)),
            dma((SWEEPS, CHUNKS)),
            dma((SWEEPS, CHUNKS)),
            dma((SWEEPS, CHUNKS)),
            dma(()),
        ],
        compiler_params=pltpu.CompilerParams(
            collective_id=0, has_side_effects=True, vmem_limit_bytes=40 * 1024 * 1024
        ),
        cost_estimate=pl.CostEstimate(
            flops=40 * SWEEPS * field.size, bytes_accessed=18 * field.size, transcendentals=0
        ),
    )(field, hess_xx, hess_yy, hess_xy, gradient)


def solution(mesh):
    cells = P("stack", "rows", None)
    fields = P(None, "stack", "rows", None)
    return jax.shard_map(
        functools.partial(on_device, mesh.shape["stack"], mesh.shape["rows"]),
        mesh=mesh, in_specs=(fields, cells, cells, cells, fields), out_specs=fields, check_vma=False,
    )
```

time: 101 us -> 53.9 us (0.53)
  the two profiles are of different devices: /device:TPU:1 before, /device:TPU:0 now
where the time goes in v1:
time: 53.9 us; the launch traced here: 53.5 us
  Pallas kernels  47.4 us (88%)
  local copies, waits for them, and re-layouts  6.13 us (11%)
    pallas_call x1, Pallas kernels, on_device(): pl.pallas_call(functools.partial(kernel, n_stack, n_rows, detour), out_sh...  47.4 us
    unnamed x11, local copies, waits for them, and re-layouts  6.13 us

profile of v1, /device:TPU:0, one launch (start us, length us, event | category | flops | bytes accessed | tf_op | source)
XLA Modules:
  0.0 53.5 jit_solution(10916011850398115320)
XLA Ops:
  0.0 0.0 copy-start
  0.0 1.1 %copy-done = f32[2,4,16,1536]{3,2,1,0:T(8,128)S(1)} copy-done((f32[2,4,16,1536]{3,2,1,0:T(8,128)S(1)}, f32[2,4,16,1536]{3,2,1,0:T(8,128)}, u32[]{:S(2)}) %copy-start) | copy-done | bytes 786456
  1.1 0.0 copy-start.1
  1.1 1.1 %copy-done.1 = f32[2,4,16,1536]{3,2,1,0:T(8,128)S(1)} copy-done((f32[2,4,16,1536]{3,2,1,0:T(8,128)S(1)}, f32[2,4,16,1536]{3,2,1,0:T(8,128)}, u32[]{:S(2)}) %copy-start.1) | copy-done | bytes 786456
  2.3 0.0 copy-start.2
  2.3 1.0 %copy-done.2 = f32[4,16,1536]{2,1,0:T(8,128)S(1)} copy-done((f32[4,16,1536]{2,1,0:T(8,128)S(1)}, f32[4,16,1536]{2,1,0:T(8,128)}, u32[]{:S(2)}) %copy-start.2) | copy-done | bytes 393240
  3.3 0.0 copy-start.3
  3.3 1.0 %copy-done.3 = f32[4,16,1536]{2,1,0:T(8,128)S(1)} copy-done((f32[4,16,1536]{2,1,0:T(8,128)S(1)}, f32[4,16,1536]{2,1,0:T(8,128)}, u32[]{:S(2)}) %copy-start.3) | copy-done | bytes 393240
  4.3 0.0 copy-start.4
  4.3 1.0 %copy-done.4 = f32[4,16,1536]{2,1,0:T(8,128)S(1)} copy-done((f32[4,16,1536]{2,1,0:T(8,128)S(1)}, f32[4,16,1536]{2,1,0:T(8,128)}, u32[]{:S(2)}) %copy-start.4) | copy-done | bytes 393240
  5.3 47.4 %shard_map.55 = f32[2,4,16,1536]{3,2,1,0:T(8,128)S(1)} custom-call(f32[2,4,16,1536]{3,2,1,0:T(8,128)S(1)} %copy-done, f32[4,16,1536]{2,1,0:T(8,128)S(1)} %copy-done.2, f32[4,16,1536]{2,1,0:T(8,128)S(1)} %copy-done.3, f32[4,16,1536]{2,1,0:T(8,128)S(1)} %copy-done.4, f32[2,4,16,1536]{3,2,1,0:T(8,128)S(1)} %copy-done.1), custom_call_target="tpu_custom_call" | custom-call | flops 47185920 | bytes 3538944 | tf_op jit(solution)/shard_map/pallas_call | solution.py:268
  52.7 0.9 %copy.7 = f32[2,4,16,1536]{3,2,1,0:T(8,128)} copy(f32[2,4,16,1536]{3,2,1,0:T(8,128)S(1)} %shard_map.55) | data formatting | bytes 1572864
Async XLA Ops:
  0.0 1.1 %copy-start = (f32[2,4,16,1536]{3,2,1,0:T(8,128)S(1)}, f32[2,4,16,1536]{3,2,1,0:T(8,128)}, u32[]{:S(2)}) copy-start(f32[2,4,16,1536]{3,2,1,0:T(8,128)} %field.1) | copy-start | bytes 2359300
  1.1 1.1 %copy-start.1 = (f32[2,4,16,1536]{3,2,1,0:T(8,128)S(1)}, f32[2,4,16,1536]{3,2,1,0:T(8,128)}, u32[]{:S(2)}) copy-start(f32[2,4,16,1536]{3,2,1,0:T(8,128)} %grad.1) | copy-start | bytes 2359300
  2.3 1.0 %copy-start.2 = (f32[4,16,1536]{2,1,0:T(8,128)S(1)}, f32[4,16,1536]{2,1,0:T(8,128)}, u32[]{:S(2)}) copy-start(f32[4,16,1536]{2,1,0:T(8,128)} %hxx.1) | copy-start | bytes 1179652
  3.3 1.0 %copy-start.3 = (f32[4,16,1536]{2,1,0:T(8,128)S(1)}, f32[4,16,1536]{2,1,0:T(8,128)}, u32[]{:S(2)}) copy-start(f32[4,16,1536]{2,1,0:T(8,128)} %hyy.1) | copy-start | bytes 1179652
  4.3 1.0 %copy-start.4 = (f32[4,16,1536]{2,1,0:T(8,128)S(1)}, f32[4,16,1536]{2,1,0:T(8,128)}, u32[]{:S(2)}) copy-start(f32[4,16,1536]{2,1,0:T(8,128)} %hxy.1) | copy-start | bytes 1179652

commit v2 on v1

--- a/solution.py
+++ b/solution.py
@@ -200,6 +200,10 @@
 
     if detour:
         over(AHEAD, pass_on)
+
+    def store(c):
+        return pltpu.make_async_copy(
+            u.at[SWEEPS, :, 2:sections + 2, :, cols(c)], out.at[:, :, :, raw_cols(c)], out_sem.at[c])
 
     top = lax.broadcasted_iota(jnp.int32, (height, cw), 0) == 0
     bottom = lax.broadcasted_iota(jnp.int32, (height, cw), 0) == height - 1
@@ -239,10 +243,11 @@
             each_section_copy(t + 1, c, start)
             send_rows(t + 1, c)
 
+        @pl.when(t == SWEEPS - 1)
+        def _():
+            store(c).start()
+
     over(SWEEPS * CHUNKS, step)
-
-    store = pltpu.make_async_copy(u.at[SWEEPS, :, 2:sections + 2, :, PAD:PAD + width], out, out_sem)
-    store.start()
 
     def drain(i):
         t, c = lax.div(i, CHUNKS), lax.rem(i, CHUNKS)
@@ -257,7 +262,7 @@
                 def _():
                     onward_copy(t, c, d).wait_send()
     over(SWEEPS * CHUNKS, drain)
-    store.wait()
+    over(CHUNKS, lambda c: store(c).wait())
 
 
 def on_device(n_stack, n_rows, field, hess_xx, hess_yy, hess_xy, gradient):
@@ -286,10 +291,10 @@
             dma((SWEEPS, CHUNKS)),
             dma((SWEEPS, CHUNKS)),
             dma((SWEEPS, CHUNKS)),
-            dma(()),
+            dma((CHUNKS,)),
         ],
         compiler_params=pltpu.CompilerParams(
-            collective_id=0, has_side_effects=True, vmem_limit_bytes=40 * 1024 * 1024
+            collective_id=0, has_side_effects=True, vmem_limit_bytes=60 * 1024 * 1024
         ),
         cost_estimate=pl.CostEstimate(
             flops=40 * SWEEPS * field.size, bytes_accessed=18 * field.size, transcendentals=0

time: 53.9 us -> 49.9 us (0.926)
  local copies, waits for them, and re-layouts: 6.13 us -> 2.07 us
    unnamed x11 -> x1, local copies, waits for them, and re-layouts: 6.13 us -> 2.07 us
where the time goes in v2:
time: 49.9 us; the launch traced here: 49.8 us
  Pallas kernels  47.7 us (96%)
  local copies, waits for them, and re-layouts  2.07 us (4%)
    pallas_call x1, Pallas kernels, on_device(): pl.pallas_call(functools.partial(kernel, n_stack, n_rows, detour), out_sh...  47.7 us
    unnamed x1, local copies, waits for them, and re-layouts  2.07 us

profile of v2, /device:TPU:0, one launch (start us, length us, event | category | flops | bytes accessed | tf_op | source)
XLA Modules:
  0.0 49.8 jit_solution(14223558638261624403)
XLA Ops:
  0.0 47.7 %shard_map.55 = f32[2,4,16,1536]{3,2,1,0:T(8,128)} custom-call(f32[2,4,16,1536]{3,2,1,0:T(8,128)} %field.1, f32[4,16,1536]{2,1,0:T(8,128)} %hxx.1, f32[4,16,1536]{2,1,0:T(8,128)} %hyy.1, f32[4,16,1536]{2,1,0:T(8,128)} %hxy.1, f32[2,4,16,1536]{3,2,1,0:T(8,128)} %grad.1), custom_call_target="tpu_custom_call" | custom-call | flops 47185920 | bytes 3538944 | tf_op jit(solution)/shard_map/pallas_call | solution.py:273
  47.7 2.1 %copy.7 = f32[2,4,16,1536]{3,2,1,0:T(8,128)} copy(f32[2,4,16,1536]{3,2,1,0:T(8,128)} %shard_map.55) | data formatting | bytes 1572864

commit v3 on v2

--- a/solution.py
+++ b/solution.py
@@ -11,7 +11,7 @@
 NEAR, FAR, PLANE, SHIFT = 1.0, 0.5, 1.0, 7.0
 PAD = 128
 CHUNKS = 4
-AHEAD = 2
+AHEAD = 1
 
 
 def kernel(n_stack, n_rows, detour, field, hxx, hyy, hxy, grad, out,
@@ -100,9 +100,11 @@
             send_sem=send_sem.at[t, c, 2 + d], recv_sem=recv_sem.at[t, c, 2 + d],
             device_id=down if d == 0 else up)
 
-    def each_section_copy(t, c, do, first=False):
+    def each_section_copy(t, c, do, first=False, only=(0, 1)):
         every, upper = slice(0, height), slice(0, half)
         for d, exists, split in ((0, has_right, is_lo), (1, has_left, is_hi)):
+            if d not in only:
+                continue
             if detour:
                 @pl.when(split)
                 def _():
@@ -237,10 +239,13 @@
             b = cb[k, :, at]
             u[t + 1, 0, 2 + k, :, cols(c)] = cc[k, :, at] * r[0] - b * r[1]
             u[t + 1, 1, 2 + k, :, cols(c)] = ca[k, :, at] * r[1] - b * r[0]
+            if k == 1 or k == sections - 1:
+                @pl.when(t < SWEEPS - 1)
+                def _():
+                    each_section_copy(t + 1, c, start, only=(1,) if k == 1 else (0,))
 
         @pl.when(t < SWEEPS - 1)
         def _():
-            each_section_copy(t + 1, c, start)
             send_rows(t + 1, c)
 
         @pl.when(t == SWEEPS - 1)

time: 49.9 us -> 48.9 us (0.980); the launches traced: 49.8 us -> 48.2 us
  Pallas kernels: 47.7 us -> 46.2 us
    pallas_call x1, Pallas kernels: 47.7 us -> 46.2 us  [on_device(): pl.pallas_call(functools.partial(kernel, n_stack, n_rows, detour), out_sh...]
where the time goes in v3:
time: 48.9 us; the launch traced here: 48.2 us
  Pallas kernels  46.2 us (94%)
  local copies, waits for them, and re-layouts  2.07 us (4%)
    pallas_call x1, Pallas kernels, on_device(): pl.pallas_call(functools.partial(kernel, n_stack, n_rows, detour), out_sh...  46.2 us
    unnamed x1, local copies, waits for them, and re-layouts  2.07 us

profile of v3, /device:TPU:0, one launch (start us, length us, event | category | flops | bytes accessed | tf_op | source)
XLA Modules:
  0.0 48.2 jit_solution(11671032154218436038)
XLA Ops:
  0.0 46.2 %shard_map.55 = f32[2,4,16,1536]{3,2,1,0:T(8,128)} custom-call(f32[2,4,16,1536]{3,2,1,0:T(8,128)} %field.1, f32[4,16,1536]{2,1,0:T(8,128)} %hxx.1, f32[4,16,1536]{2,1,0:T(8,128)} %hyy.1, f32[4,16,1536]{2,1,0:T(8,128)} %hxy.1, f32[2,4,16,1536]{3,2,1,0:T(8,128)} %grad.1), custom_call_target="tpu_custom_call" | custom-call | flops 47185920 | bytes 3538944 | tf_op jit(solution)/shard_map/pallas_call | solution.py:278
  46.2 2.1 %copy.7 = f32[2,4,16,1536]{3,2,1,0:T(8,128)} copy(f32[2,4,16,1536]{3,2,1,0:T(8,128)} %shard_map.55) | data formatting | bytes 1572864

commit v4 on v3

--- a/solution.py
+++ b/solution.py
@@ -128,9 +128,11 @@
         if other is not None:
             other.wait_send()
 
-    def await_sections(t, c):
+    def await_sections(t, c, only):
         every, upper = slice(0, height), slice(0, half)
         for d, exists, split in ((0, has_left, is_hi), (1, has_right, is_lo)):
+            if d != only:
+                continue
             if detour:
                 @pl.when(split)
                 def _():
@@ -220,9 +222,12 @@
             @pl.when(exists)
             def _():
                 row_copy(t, c, d).wait_recv()
-        await_sections(t, c)
         at = raw_cols(c)
         for k in range(sections):
+            if k == 0:
+                await_sections(t, c, 0)
+            if k == sections - 2:
+                await_sections(t, c, 1)
             r = []
             for comp in range(2):
                 wide = u[t, comp, 2 + k, :, pl.ds(pl.multiple_of(c * cw, 128), cw + 2 * PAD)]

time: 48.9 us -> 48.7 us (level)
  Pallas kernels: 46.2 us -> 45.7 us
    pallas_call x1, Pallas kernels: 46.2 us -> 45.7 us  [on_device(): pl.pallas_call(functools.partial(kernel, n_stack, n_rows, detour), out_sh...]
where the time goes in v4:
time: 48.7 us; the launch traced here: 47.7 us
  Pallas kernels  45.7 us (94%)
  local copies, waits for them, and re-layouts  2.07 us (4%)
    pallas_call x1, Pallas kernels, on_device(): pl.pallas_call(functools.partial(kernel, n_stack, n_rows, detour), out_sh...  45.7 us
    unnamed x1, local copies, waits for them, and re-layouts  2.07 us

profile of v4, /device:TPU:0, one launch (start us, length us, event | category | flops | bytes accessed | tf_op | source)
XLA Modules:
  0.0 47.7 jit_solution(7866563350979760137)
XLA Ops:
  0.0 45.7 %shard_map.55 = f32[2,4,16,1536]{3,2,1,0:T(8,128)} custom-call(f32[2,4,16,1536]{3,2,1,0:T(8,128)} %field.1, f32[4,16,1536]{2,1,0:T(8,128)} %hxx.1, f32[4,16,1536]{2,1,0:T(8,128)} %hyy.1, f32[4,16,1536]{2,1,0:T(8,128)} %hxy.1, f32[2,4,16,1536]{3,2,1,0:T(8,128)} %grad.1), custom_call_target="tpu_custom_call" | custom-call | flops 47185920 | bytes 3538944 | tf_op jit(solution)/shard_map/pallas_call | solution.py:283
  45.7 2.1 %copy.7 = f32[2,4,16,1536]{3,2,1,0:T(8,128)} copy(f32[2,4,16,1536]{3,2,1,0:T(8,128)} %shard_map.55) | data formatting | bytes 1572864
